TPU v7x, 32 devices: a whole 2x2x4 slice. The times are simulated.
32 devices in a mesh: inner: 16 (over z, y, x), outer: 2 (over core).
Axes of the slice: x: 2, y: 2, z: 4, core: 2. Of those that a mesh axis runs over, the one named last changes fastest.
Arguments:
- feats_first: bfloat16 [2, 4096, 2048], P('outer', 'inner'), may hold values from -4 to 8
- feats_second: bfloat16 [2, 4096, 2048], P('outer', 'inner'), may hold values from -4 to 8
- expander: bfloat16 [2048, 1024], P('inner'), may hold values from -0.125 to 0.125
- tile_count: int32 [2, 16], replicated, may hold values from 64 to 256, as said below
- match_dev: int32 [2, 4096, 1], P('outer', 'inner'), may hold values from 0 to 15; in each aligned block of 256 rows (0 to 255, 256 to 511, ..., all dimensions but the last counted through in order) at most 48 rows name the same one
- match_tile: int32 [2, 4096], P('outer', 'inner'), may hold values from 0 to 255
Outputs:
- covariance: float32 [1024, 1024], P('inner')
- invariance: float32 [2, 4096], P('outer', 'inner')
Inputs may be any that keep to these rules, and one draw needn't show every extreme that they name: `tile_count`: for every slide some device has all 256 tiles live; the others at least a quarter. `match_dev`: at most 48 tiles of one device name the same device.
All inputs are finite; a program needn't handle non-finite values.
Results may differ from a plain program's by a relative error of at most 0.00135.
Values may be sent and summed in bfloat16 or wider, within the bound.
A program may use at most 64 MiB of HBM per device.

v0:
```python
import jax
import jax.numpy as jnp
from jax import lax
from jax.sharding import PartitionSpec as P


def shards(feats_first, feats_second, expander, tile_count, match_dev, match_tile):
    first_rows = feats_first[0]
    second_rows = feats_second[0]
    tile_rows = first_rows.shape[0]
    expand_width = expander.shape[1]
    group_size = lax.axis_size("inner")
    capacity = max(2, 3 * tile_rows // group_size)
    inner_pos = lax.axis_index("inner")
    outer_pos = lax.axis_index("outer")
    piece = lax.all_gather(expander, "inner", axis=0, tiled=True)
    first_acc = jnp.dot(first_rows, piece, preferred_element_type=jnp.float32)
    second_acc = jnp.dot(second_rows, piece, preferred_element_type=jnp.float32)
    first_embed = first_acc.astype(jnp.bfloat16)
    second_embed = second_acc.astype(jnp.bfloat16)
    counts = lax.dynamic_index_in_dim(tile_count, outer_pos, 0, keepdims=False)
    own_count = lax.dynamic_index_in_dim(counts, inner_pos, 0, keepdims=False)
    row_index = jnp.arange(tile_rows, dtype=jnp.int32)
    live = row_index < own_count
    target_dev = match_dev[0, :, 0]
    target_tile = match_tile[0]
    onehot = (target_dev[:, None] == jnp.arange(group_size, dtype=jnp.int32)[None, :]).astype(
        jnp.int32
    )
    slot_pos = jnp.sum((jnp.cumsum(onehot, axis=0) - 1) * onehot, axis=1)
    send_rows = (
        jnp.zeros((group_size, capacity, expand_width), jnp.bfloat16)
        .at[target_dev, slot_pos]
        .set(first_embed)
    )
    send_tiles = (
        jnp.zeros((group_size, capacity), jnp.int32).at[target_dev, slot_pos].set(target_tile)
    )
    recv_rows, recv_tiles = (
        lax.all_to_all(send_rows, "inner", split_axis=0, concat_axis=0, tiled=True),
        lax.all_to_all(send_tiles, "inner", split_axis=0, concat_axis=0, tiled=True),
    )
    partner = second_embed[recv_tiles]
    diff = recv_rows.astype(jnp.float32) - partner.astype(jnp.float32)
    distance = jnp.where(recv_tiles < own_count, jnp.mean(diff * diff, axis=-1), jnp.float32(0.0))
    returned = lax.all_to_all(distance, "inner", split_axis=0, concat_axis=0, tiled=True)
    dest_count = counts[target_dev]
    valid = live & (target_tile < dest_count)
    invariance = jnp.where(valid, returned[target_dev, slot_pos], jnp.float32(0.0))
    masked = jnp.where(live[:, None], first_embed, jnp.zeros_like(first_embed))
    column_total = lax.psum(jnp.sum(masked.astype(jnp.float32), axis=0), ("inner", "outer"))
    total = jnp.sum(tile_count).astype(jnp.float32)
    share_rows = expand_width // group_size
    local_share = lax.psum_scatter(
        lax.dot_general(
            masked, masked, (((0,), (0,)), ((), ())), preferred_element_type=jnp.float32
        ),
        "inner",
        scatter_dimension=0,
        tiled=True,
    )
    gram_share = lax.psum(local_share, "outer")
    own_sums = lax.dynamic_slice_in_dim(column_total, inner_pos * share_rows, share_rows, 0)
    covariance = (gram_share - own_sums[:, None] * column_total[None, :] / total) / (total - 1.0)
    return (covariance, invariance[None, :])


def solution(mesh):
    return jax.shard_map(
        shards,
        mesh=mesh,
        in_specs=(
            P("outer", "inner", None),
            P("outer", "inner", None),
            P("inner", None),
            P(),
            P("outer", "inner", None),
            P("outer", "inner"),
        ),
        out_specs=(P("inner", None), P("outer", "inner")),
        check_vma=False,
    )
```

profile of v0, /device:TPU:0, one launch (start us, length us, event | category | flops | bytes accessed | tf_op | source)
XLA Modules:
  0.0 292.9 jit_solution(2286077928159644080)
XLA Ops:
  7.2 0.7 all-gather.2.cloned.1.call-update
  8.0 1.3 dynamic_slice.11
  9.3 0.6 iota_compare_fusion.2
  10.0 79.6 %all-gather.2.cloned.1.call-done = bf16[2048,1024]{1,0:T(8,128)(2,1)} async-done(((bf16[128,1024]{1,0:T(8,128)(2,1)}), bf16[2048,1024]{1,0:T(8,128)(2,1)}) %all-gather.2.cloned.1.call-update) | async-done | bytes 4194320 | tf_op jit(solution)/shard_map/all_gather | solution.py:16
  89.6 3.4 %convert_reduce_fusion = (f32[1024]{0:T(1024)S(1)}, bf16[256,1024]{1,0:T(8,128)(2,1)S(1)}) fusion(pred[256]{0:T(512)(128)(4,1)S(1)} %iota_compare_fusion.2, bf16[2048,1024]{1,0:T(8,128)(2,1)} %all-gather.2.cloned.1.call-done, bf16[1,256,2048]{2,1,0:T(8,128)(2,1)S(1)} %copy-done), kind=kOutput, calls=%fused_computation.11 | convolution fusion | flops 1074789376 | bytes 5771520 | tf_op jit(solution)/shard_map/dot_general | solution.py:17
  93.1 2.8 fusion.4
  95.9 0.6 copy-done.1
  96.5 0.6 reduce-window.6
  97.1 0.2 slice_reduce_fusion
  97.3 0.7 fusion.11
  98.1 0.1 fusion.6
  98.1 4.3 %compare_select_fusion.4 = (s32[256,1]{0,1:T(1,128)S(1)}, s32[256,1]{0,1:T(1,128)S(1)}) fusion(s32[]{:T(128)} %bitcast.12, s32[]{:T(128)} %bitcast.13, s32[]{:T(128)} %bitcast.14, s32[]{:T(128)} %bitcast.15, s32[]{:T(128)} %bitcast.16, s32[]{:T(128)} %bitcast.18, s32[]{:T(128)} %bitcast.17, s32[1,256,1]{1,2,0:T(1,128)S(1)} %copy-done.1), kind=kLoop, calls=%fused_computation.38 | loop fusion | flops 3840 | bytes 3100 | tf_op jit(solution)/shard_map/gather | solution.py:47
  102.4 0.6 broadcast.105
  103.0 36.1 %scatter_fusion = s32[16,48]{1,0:T(8,128)} fusion(s32[16,48]{1,0:T(8,128)} %broadcast.105, s32[256]{0:T(256)S(1)} %bitcast.67, s32[256]{0:T(256)S(1)} %bitcast.75), kind=kCustom, calls=%fused_computation.2 | custom fusion | bytes 5120 | tf_op jit(solution)/shard_map/scatter | solution.py:37
  139.2 4.4 %all-to-all-start = ((s32[16,1,48]{2,1,0:T(1,128)}), s32[16,1,48]{2,1,0:T(1,128)S(1)}, u32[]{:S(2)}, u32[]{:S(2)}) async-start(s32[16,1,48]{2,1,0:T(1,128)} %bitcast.28), calls=%async_computation.1 | async-start | bytes 16384 | tf_op jit(solution)/shard_map/all_to_all | solution.py:41
  143.6 1.4 broadcast_in_dim.22
  145.0 36.8 %scatter_fusion.1 = bf16[16,48,1024]{2,1,0:T(8,128)(2,1)} fusion(bf16[16,48,1024]{2,1,0:T(8,128)(2,1)} %broadcast_in_dim.22, s32[256]{0:T(256)S(1)} %bitcast.68, bf16[256,1024]{1,0:T(8,128)(2,1)S(1)} %get-tuple-element.32), kind=kCustom, calls=%fused_computation.3 | custom fusion | bytes 1574912 | tf_op jit(solution)/shard_map/scatter | solution.py:34
  181.8 7.1 %all-to-all-start.1 = ((bf16[16,48,1024]{2,1,0:T(8,128)(2,1)}), bf16[16,48,1024]{2,1,0:T(8,128)(2,1)S(1)}, u32[]{:S(2)}, u32[]{:S(2)}) async-start(bf16[16,48,1024]{2,1,0:T(8,128)(2,1)} %scatter_fusion.1), calls=%async_computation.2 | async-start | bytes 3145728 | tf_op jit(solution)/shard_map/all_to_all | solution.py:40
  189.0 0.1 reshape.148
  189.0 3.8 %convolution_convert_fusion = bf16[256,1024]{1,0:T(8,128)(2,1)S(1)} fusion(bf16[2048,1024]{1,0:T(8,128)(2,1)} %all-gather.2.cloned.1.call-done, bf16[1,256,2048]{2,1,0:T(8,128)(2,1)} %param.7), kind=kOutput, calls=%fused_computation.7 | convolution fusion | flops 1074003968 | bytes 5767168 | tf_op jit(solution)/shard_map/dot_general | solution.py:18
  192.8 3.6 %gather_fusion = bf16[768,1024]{1,0:T(8,128)(2,1)} fusion(bf16[256,1024]{1,0:T(8,128)(2,1)S(1)} %convolution_convert_fusion, s32[1024]{0:T(1024)S(1)} %pad_clamp_fusion), kind=kCustom, calls=%fused_computation | custom fusion | bytes 3148800 | tf_op jit(solution)/shard_map/gather | solution.py:43
  196.4 26.0 %all-to-all-done.1 = bf16[16,48,1024]{2,1,0:T(8,128)(2,1)S(1)} async-done(((bf16[16,48,1024]{2,1,0:T(8,128)(2,1)}), bf16[16,48,1024]{2,1,0:T(8,128)(2,1)S(1)}, u32[]{:S(2)}, u32[]{:S(2)}) %all-to-all-start.1) | async-done | bytes 1572896 | tf_op jit(solution)/shard_map/all_to_all | solution.py:40
  222.4 2.0 fusion.1
  224.4 1.2 compare_select_fusion
  225.6 7.3 %all-to-all-start.2 = ((f32[16,1,48]{2,1,0:T(1,128)}), f32[16,1,48]{2,1,0:T(1,128)S(1)}, u32[]{:S(2)}, u32[]{:S(2)}) async-start(f32[16,1,48]{2,1,0:T(1,128)} %compare_select_fusion), calls=%async_computation.3 | async-start | bytes 16384 | tf_op jit(solution)/shard_map/all_to_all | solution.py:46
  233.0 0.7 all-reduce.2.cloned.1.call-update
  233.7 5.6 %select_select_fusion = s32[256]{0:T(256)S(1)} fusion(pred[256]{0:T(512)(128)(4,1)S(1)} %get-tuple-element.10, pred[256]{0:T(512)(128)(4,1)S(1)} %get-tuple-element.9, pred[256]{0:T(512)(128)(4,1)S(1)} %get-tuple-element.8, pred[256]{0:T(512)(128)(4,1)S(1)} %get-tuple-element.7, pred[256]{0:T(512)(128)(4,1)S(1)} %get-tuple-element.6, ...), kind=kLoop, calls=%fused_computation.49 | loop fusion | flops 2304 | bytes 4388 | tf_op jit(solution)/shard_map/gather | solution.py:47
  239.3 0.6 reduce_sum.39
  240.6 40.7 %psum.15 = f32[1024]{0:T(1024)S(1)} all-reduce(f32[1024]{0:T(1024)S(1)} %get-tuple-element.31), channel_id=1, replica_groups=mesh['inner'=16,'outer'=2] {'inner','outer'}, use_global_device_ids=true, to_apply=%region_3.4 | all-reduce | flops 1024 | bytes 8192 | tf_op jit(solution)/shard_map/psum | solution.py:51
  281.4 1.9 gather_fusion.1
  283.4 1.2 and_select_fusion
  284.6 1.8 subtract_divide_fusion
  (25 shorter events, 0.4 us)
Async XLA Ops:
  7.2 82.4 %copy-start = (bf16[1,256,2048]{2,1,0:T(8,128)(2,1)S(1)}, bf16[1,256,2048]{2,1,0:T(8,128)(2,1)}, u32[]{:S(2)}) copy-start(bf16[1,256,2048]{2,1,0:T(8,128)(2,1)} %param.6) | copy-start | bytes 3145732
  7.2 82.4 %all-gather.2.cloned.1.call-start = ((), (), s32[]{:S(2)}) async-start(), calls=%async_computation.4 | async-start | bytes 4456448 | tf_op jit(solution)/shard_map/all_gather | solution.py:16
  7.9 225.1 %reduce-scatter.2.cloned.1.call-start = ((), (), s32[]{:S(2)}) async-start(), calls=%async_computation.5 | async-start | bytes 4456448 | tf_op jit(solution)/shard_map/reduce_scatter | solution.py:54
  95.8 0.7 copy-start.1
  95.8 1.5 copy-start.3
  95.8 7.2 %copy-start.2 = (s32[1,256]{1,0:T(1,128)S(1)}, s32[1,256]{1,0:T(1,128)}, u32[]{:S(2)}) copy-start(s32[1,256]{1,0:T(1,128)} %param.11) | copy-start | bytes 3076
  139.2 42.6 %all-to-all-start = ((s32[16,1,48]{2,1,0:T(1,128)}), s32[16,1,48]{2,1,0:T(1,128)S(1)}, u32[]{:S(2)}, u32[]{:S(2)}) async-start(s32[16,1,48]{2,1,0:T(1,128)} %bitcast.28), calls=%async_computation.1 | async-start | bytes 16384 | tf_op jit(solution)/shard_map/all_to_all | solution.py:41
  181.8 40.6 %all-to-all-start.1 = ((bf16[16,48,1024]{2,1,0:T(8,128)(2,1)}), bf16[16,48,1024]{2,1,0:T(8,128)(2,1)S(1)}, u32[]{:S(2)}, u32[]{:S(2)}) async-start(bf16[16,48,1024]{2,1,0:T(8,128)(2,1)} %scatter_fusion.1), calls=%async_computation.2 | async-start | bytes 3145728 | tf_op jit(solution)/shard_map/all_to_all | solution.py:40
  225.6 55.8 %all-to-all-start.2 = ((f32[16,1,48]{2,1,0:T(1,128)}), f32[16,1,48]{2,1,0:T(1,128)S(1)}, u32[]{:S(2)}, u32[]{:S(2)}) async-start(f32[16,1,48]{2,1,0:T(1,128)} %compare_select_fusion), calls=%async_computation.3 | async-start | bytes 16384 | tf_op jit(solution)/shard_map/all_to_all | solution.py:46
  233.0 51.6 %all-reduce.2.cloned.1.call-start = ((), (), s32[]{:S(2)}) async-start(), calls=%async_computation.6 | async-start | bytes 524288 | tf_op jit(solution)/shard_map/psum | solution.py:62
Sparse Core Ops, SparseCore 0:
  10.8 78.7 all-gather.1
  96.0 93.7 reduce-scatter.1
  236.1 19.5 all-reduce.1
where the time goes:
time: 296 us; the launch traced here: 293 us
  waiting for transfers between devices  107 us (36%)
  local copies, waits for them, and re-layouts  83.5 us (28%)
  blocking collectives  40.7 us (14%)
  starting transfers between devices  18.9 us (6%)
  other arithmetic  18.1 us (6%)
  between operations  14.5 us (5%)
  matrix products  10 us (3%)
    all_gather x1, waiting for transfers between devices, shards(): piece = lax.all_gather(expander, 'inner', axis=0, tiled=True)  79.6 us
    psum x1, blocking collectives, shards(): lax.psum(jnp.sum(masked.astype(jnp.float32), axis=0), ('inner', 'outer'))  40.7 us
    scatter x1, local copies, waits for them, and re-layouts, shards(): send_rows = jnp.zeros((group_size, capacity, expand_width), jnp.bfloat16)...  36.8 us
    scatter x1, local copies, waits for them, and re-layouts, shards(): jnp.zeros((group_size, capacity), jnp.int32).at[target_dev, slot_pos]  36.1 us
    all_to_all x1, waiting for transfers between devices, shards(): lax.all_to_all(send_rows, 'inner', split_axis=0, concat_axis=0, tiled=True)  26 us
    gather x3, other arithmetic, shards(): dest_count = counts[target_dev]  9.95 us
    all_to_all x1, starting transfers between devices, shards(): lax.all_to_all(distance, 'inner', split_axis=0, concat_axis=0, tiled=True)  7.3 us
    all_to_all x1, starting transfers between devices, shards(): lax.all_to_all(send_rows, 'inner', split_axis=0, concat_axis=0, tiled=True)  7.08 us
  transfers between devices with their start and end apart: 6, of which 2 were waited for; matrix products, arithmetic and copies ran while one was open for 35% of the time, Pallas kernels for 0%

commit v1 on v0

--- a/solution.py
+++ b/solution.py
@@ -2,6 +2,29 @@
 import jax.numpy as jnp
 from jax import lax
 from jax.sharding import PartitionSpec as P
+
+
+def cut_along(value, dim, length):
+    dims = value.shape
+    blocks = value.reshape(*dims[:dim], length, dims[dim] // length, *dims[dim + 1 :])
+    return jnp.moveaxis(blocks, dim, 0)
+
+
+def in_order(blocks, dim):
+    blocks = jnp.moveaxis(blocks, 0, dim)
+    dims = blocks.shape
+    return blocks.reshape(*dims[:dim], dims[dim] * dims[dim + 1], *dims[dim + 2 :])
+
+
+def pairwise_exchange(array, axis, split_dim, concat_dim):
+    count, mine = (lax.axis_size(axis), lax.axis_index(axis))
+    blocks = cut_along(array, split_dim, count)
+    gathered = [blocks[mine]]
+    for lap in range(1, count):
+        sent = blocks[mine ^ lap]
+        gathered.append(lax.ppermute(sent, axis, [(i, i ^ lap) for i in range(count)]))
+    blocks = jnp.stack(gathered)[mine ^ jnp.arange(count)]
+    return in_order(blocks, concat_dim)
 
 
 def shards(feats_first, feats_second, expander, tile_count, match_dev, match_tile):
@@ -37,7 +60,7 @@
         jnp.zeros((group_size, capacity), jnp.int32).at[target_dev, slot_pos].set(target_tile)
     )
     recv_rows, recv_tiles = (
-        lax.all_to_all(send_rows, "inner", split_axis=0, concat_axis=0, tiled=True),
+        pairwise_exchange(send_rows, "inner", 0, 0),
         lax.all_to_all(send_tiles, "inner", split_axis=0, concat_axis=0, tiled=True),
     )
     partner = second_embed[recv_tiles]

time: 296 us -> 329 us (1.11)
  waiting for transfers between devices: 107 us -> 144 us
  local copies, waits for them, and re-layouts: 83.5 us -> 69.1 us
  starting transfers between devices: 18.9 us -> 28.6 us
    ppermute x0 -> x15, waiting for transfers between devices: none -> 56.7 us  [pairwise_exchange(): lax.ppermute(sent, axis, [(i, i ^ lap) for i in range(count)])]
    all_to_all x1 -> x0, waiting for transfers between devices: 26 us -> none  [shards(): lax.all_to_all(send_rows, 'inner', split_axis=0, concat_axis=0, tiled=True)]
    ppermute x0 -> x15, starting transfers between devices: none -> 20.4 us  [pairwise_exchange(): lax.ppermute(sent, axis, [(i, i ^ lap) for i in range(count)])]
    scatter x1, local copies, waits for them, and re-layouts: 36.8 us -> 16.6 us  [shards(): send_rows = jnp.zeros((group_size, capacity, expand_width), jnp.bfloat16)...]
    all_to_all x1 -> x0, starting transfers between devices: 7.08 us -> none  [shards(): lax.all_to_all(send_rows, 'inner', split_axis=0, concat_axis=0, tiled=True)]
    all_to_all x1, waiting for transfers between devices: 0.01 us -> 5.97 us  [shards(): lax.all_to_all(send_tiles, 'inner', split_axis=0, concat_axis=0, tiled=True)]
    all_to_all x1, starting transfers between devices: 7.3 us -> 3.67 us  [shards(): lax.all_to_all(distance, 'inner', split_axis=0, concat_axis=0, tiled=True)]
    gather x0 -> x1, local copies, waits for them, and re-layouts: none -> 3.49 us  [pairwise_exchange(): blocks = jnp.stack(gathered)[mine ^ jnp.arange(count)]]
  transfers between devices with their start and end apart: 6 -> 20, of which waited for: 2 -> 13; matrix products, arithmetic and copies ran while one was open for 35% -> 27% of each run, Pallas kernels for 0% -> 0%
where the time goes in v1:
time: 329 us; the launch traced here: 328 us
  waiting for transfers between devices  144 us (44%)
  local copies, waits for them, and re-layouts  69.1 us (21%)
  blocking collectives  40.7 us (12%)
  starting transfers between devices  28.6 us (9%)
  other arithmetic  20.5 us (6%)
  between operations  14.8 us (4%)
  matrix products  10.3 us (3%)
    all_gather x1, waiting for transfers between devices, shards(): piece = lax.all_gather(expander, 'inner', axis=0, tiled=True)  79.6 us
    ppermute x15, waiting for transfers between devices, pairwise_exchange(): lax.ppermute(sent, axis, [(i, i ^ lap) for i in range(count)])  56.7 us
    psum x1, blocking collectives, shards(): lax.psum(jnp.sum(masked.astype(jnp.float32), axis=0), ('inner', 'outer'))  40.7 us
    scatter x1, local copies, waits for them, and re-layouts, shards(): jnp.zeros((group_size, capacity), jnp.int32).at[target_dev, slot_pos]  36.1 us
    ppermute x15, starting transfers between devices, pairwise_exchange(): lax.ppermute(sent, axis, [(i, i ^ lap) for i in range(count)])  20.4 us
    scatter x1, local copies, waits for them, and re-layouts, shards(): send_rows = jnp.zeros((group_size, capacity, expand_width), jnp.bfloat16)...  16.6 us
    gather x3, other arithmetic, shards(): dest_count = counts[target_dev]  11.1 us
  transfers between devices with their start and end apart: 20, of which 13 were waited for; matrix products, arithmetic and copies ran while one was open for 27% of the time, Pallas kernels for 0%

profile of v1, /device:TPU:0, one launch (start us, length us, event | category | flops | bytes accessed | tf_op | source)
XLA Modules:
  0.0 327.7 jit_solution(13470645601744815664)
XLA Ops:
  9.9 79.6 %all-gather.2.cloned.1.call-done = bf16[2048,1024]{1,0:T(8,128)(2,1)} async-done(((bf16[128,1024]{1,0:T(8,128)(2,1)}), bf16[2048,1024]{1,0:T(8,128)(2,1)}) %all-gather.2.cloned.1.call-update) | async-done | bytes 4194320 | tf_op jit(solution)/shard_map/all_gather | solution.py:39
  89.6 4.0 %convert_reduce_fusion = (f32[1024]{0:T(1024)}, bf16[256,1024]{1,0:T(8,128)(2,1)S(1)}) fusion(pred[256]{0:T(512)(128)(4,1)S(1)} %iota_compare_fusion.2, bf16[2048,1024]{1,0:T(8,128)(2,1)} %all-gather.2.cloned.1.call-done, bf16[1,256,2048]{2,1,0:T(8,128)(2,1)S(1)} %copy-done), kind=kOutput, calls=%fused_computation.12 | convolution fusion | flops 1074789376 | bytes 5771520 | tf_op jit(solution)/shard_map/dot_general | solution.py:40
  93.6 2.8 fusion.4
  98.7 4.8 %compare_select_fusion.4 = (s32[256,1]{0,1:T(1,128)}, s32[256,1]{0,1:T(1,128)S(1)}) fusion(s32[]{:T(128)} %bitcast.12, s32[]{:T(128)} %bitcast.13, s32[]{:T(128)} %bitcast.14, s32[]{:T(128)} %bitcast.15, s32[]{:T(128)} %bitcast.16, s32[]{:T(128)} %bitcast.18, s32[]{:T(128)} %bitcast.17, s32[1,256,1]{1,2,0:T(1,128)S(1)} %copy-done.7), kind=kLoop, calls=%fused_computation.72 | loop fusion | flops 3840 | bytes 3100 | tf_op jit(solution)/shard_map/gather | solution.py:70
  104.2 36.1 %scatter_fusion = s32[16,48]{1,0:T(8,128)} fusion(s32[16,48]{1,0:T(8,128)} %broadcast.132, s32[256]{0:T(256)S(1)} %bitcast.102, s32[256]{0:T(256)S(1)} %bitcast.111), kind=kCustom, calls=%fused_computation.3 | custom fusion | bytes 5120 | tf_op jit(solution)/shard_map/scatter | solution.py:60
  140.3 4.4 %all-to-all-start = ((s32[16,1,48]{2,1,0:T(1,128)}), s32[16,1,48]{2,1,0:T(1,128)S(1)}, u32[]{:S(2)}, u32[]{:S(2)}) async-start(s32[16,1,48]{2,1,0:T(1,128)} %bitcast.28), calls=%async_computation.1 | async-start | bytes 16384 | tf_op jit(solution)/shard_map/all_to_all | solution.py:64
  145.9 6.0 %all-to-all-done = s32[16,1,48]{2,1,0:T(1,128)S(1)} async-done(((s32[16,1,48]{2,1,0:T(1,128)}), s32[16,1,48]{2,1,0:T(1,128)S(1)}, u32[]{:S(2)}, u32[]{:S(2)}) %all-to-all-start) | async-done | bytes 3104 | tf_op jit(solution)/shard_map/all_to_all | solution.py:64
  152.8 16.6 %scatter_fusion.1 = bf16[16,48,1024]{2,1,0:T(8,128)(2,1)S(1)} fusion(bf16[16,48,1024]{2,1,0:T(8,128)(2,1)S(1)} %broadcast_in_dim.19, s32[256]{0:T(256)S(1)} %bitcast.103, bf16[256,1024]{1,0:T(8,128)(2,1)S(1)} %get-tuple-element.47), kind=kCustom, calls=%fused_computation.4 | custom fusion | bytes 1574912 | tf_op jit(solution)/shard_map/scatter | solution.py:57
  171.5 3.9 %collective-permute-start.13 = (bf16[1,48,1024]{2,1,0:T(8,128)(2,1)}, bf16[1,48,1024]{2,1,0:T(8,128)(2,1)S(1)}, u32[]{:S(2)}, u32[]{:S(2)}) collective-permute-start(bf16[1,48,1024]{2,1,0:T(8,128)(2,1)} %get-tuple-element.16), channel_id=1, source_target_pairs={{0,28},{2,30},{4,24},{6,26},{8,20},{10,22},{12,16},{14,18},{16,12}... | collective-permute-start | bytes 294920 | tf_op jit(solution)/shard_map/ppermute | solution.py:25
  175.4 1.6 collective-permute-start.12
  177.0 3.1 collective-permute-start.11
  180.6 3.5 %convolution_convert_fusion = bf16[256,1024]{1,0:T(8,128)(2,1)S(1)} fusion(bf16[2048,1024]{1,0:T(8,128)(2,1)} %all-gather.2.cloned.1.call-done, bf16[1,256,2048]{2,1,0:T(8,128)(2,1)S(1)} %copy-done.23), kind=kOutput, calls=%fused_computation.8 | convolution fusion | flops 1074003968 | bytes 5767168 | tf_op jit(solution)/shard_map/dot_general | solution.py:41
  184.1 3.6 %gather_fusion.1 = bf16[768,1024]{1,0:T(8,128)(2,1)} fusion(bf16[256,1024]{1,0:T(8,128)(2,1)S(1)} %convolution_convert_fusion, s32[1024]{0:T(1024)S(1)} %copy-done.6), kind=kCustom, calls=%fused_computation.1 | custom fusion | bytes 3148800 | tf_op jit(solution)/shard_map/gather | solution.py:66
  187.7 1.8 collective-permute-done
  189.5 2.1 collective-permute-start.1
  192.5 2.7 collective-permute-done.1
  196.4 4.5 %collective-permute-done.2 = bf16[1,48,1024]{2,1,0:T(8,128)(2,1)S(1)} collective-permute-done((bf16[1,48,1024]{2,1,0:T(8,128)(2,1)}, bf16[1,48,1024]{2,1,0:T(8,128)(2,1)S(1)}, u32[]{:S(2)}, u32[]{:S(2)}) %collective-permute-start.2) | collective-permute-done | bytes 98336 | tf_op jit(solution)/shard_map/ppermute | solution.py:25
  200.9 5.3 %collective-permute-done.3 = bf16[1,48,1024]{2,1,0:T(8,128)(2,1)S(1)} collective-permute-done((bf16[1,48,1024]{2,1,0:T(8,128)(2,1)}, bf16[1,48,1024]{2,1,0:T(8,128)(2,1)S(1)}, u32[]{:S(2)}, u32[]{:S(2)}) %collective-permute-start.3) | collective-permute-done | bytes 98336 | tf_op jit(solution)/shard_map/ppermute | solution.py:25
  207.7 4.2 %collective-permute-done.4 = bf16[1,48,1024]{2,1,0:T(8,128)(2,1)S(1)} collective-permute-done((bf16[1,48,1024]{2,1,0:T(8,128)(2,1)}, bf16[1,48,1024]{2,1,0:T(8,128)(2,1)S(1)}, u32[]{:S(2)}, u32[]{:S(2)}) %collective-permute-start.4) | collective-permute-done | bytes 98336 | tf_op jit(solution)/shard_map/ppermute | solution.py:25
  213.3 5.1 %collective-permute-done.5 = bf16[1,48,1024]{2,1,0:T(8,128)(2,1)S(1)} collective-permute-done((bf16[1,48,1024]{2,1,0:T(8,128)(2,1)}, bf16[1,48,1024]{2,1,0:T(8,128)(2,1)S(1)}, u32[]{:S(2)}, u32[]{:S(2)}) %collective-permute-start.5) | collective-permute-done | bytes 98336 | tf_op jit(solution)/shard_map/ppermute | solution.py:25
  219.9 5.1 %collective-permute-done.6 = bf16[1,48,1024]{2,1,0:T(8,128)(2,1)S(1)} collective-permute-done((bf16[1,48,1024]{2,1,0:T(8,128)(2,1)}, bf16[1,48,1024]{2,1,0:T(8,128)(2,1)S(1)}, u32[]{:S(2)}, u32[]{:S(2)}) %collective-permute-start.6) | collective-permute-done | bytes 98336 | tf_op jit(solution)/shard_map/ppermute | solution.py:25
  226.3 6.6 %collective-permute-done.7 = bf16[1,48,1024]{2,1,0:T(8,128)(2,1)S(1)} collective-permute-done((bf16[1,48,1024]{2,1,0:T(8,128)(2,1)}, bf16[1,48,1024]{2,1,0:T(8,128)(2,1)S(1)}, u32[]{:S(2)}, u32[]{:S(2)}) %collective-permute-start.7) | collective-permute-done | bytes 98336 | tf_op jit(solution)/shard_map/ppermute | solution.py:25
  233.8 8.2 %collective-permute-done.8 = bf16[1,48,1024]{2,1,0:T(8,128)(2,1)S(1)} collective-permute-done((bf16[1,48,1024]{2,1,0:T(8,128)(2,1)S(1)}, bf16[1,48,1024]{2,1,0:T(8,128)(2,1)S(1)}, u32[]{:S(2)}, u32[]{:S(2)}) %collective-permute-start.8) | collective-permute-done | bytes 98336 | tf_op jit(solution)/shard_map/ppermute | solution.py:25
  242.0 6.4 %collective-permute-done.9 = bf16[1,48,1024]{2,1,0:T(8,128)(2,1)S(1)} collective-permute-done((bf16[1,48,1024]{2,1,0:T(8,128)(2,1)S(1)}, bf16[1,48,1024]{2,1,0:T(8,128)(2,1)S(1)}, u32[]{:S(2)}, u32[]{:S(2)}) %collective-permute-start.9) | collective-permute-done | bytes 98336 | tf_op jit(solution)/shard_map/ppermute | solution.py:25
  248.9 6.8 %collective-permute-done.10 = bf16[1,48,1024]{2,1,0:T(8,128)(2,1)S(1)} collective-permute-done((bf16[1,48,1024]{2,1,0:T(8,128)(2,1)S(1)}, bf16[1,48,1024]{2,1,0:T(8,128)(2,1)S(1)}, u32[]{:S(2)}, u32[]{:S(2)}) %collective-permute-start.10) | collective-permute-done | bytes 98336 | tf_op jit(solution)/shard_map/ppermute | solution.py:25
  257.1 3.5 %gather_fusion = bf16[16,48,1024]{2,1,0:T(8,128)(2,1)} fusion(bf16[16,48,1024]{2,1,0:T(8,128)(2,1)} %bitcast.106, s32[1024]{0:T(1024)} %pad_clamp_fusion.1), kind=kCustom, calls=%fused_computation | custom fusion | bytes 3145792 | tf_op jit(solution)/shard_map/gather | solution.py:26
  260.7 2.0 fusion.1
  264.0 3.7 %all-to-all-start.1 = ((f32[16,1,48]{2,1,0:T(1,128)}), f32[16,1,48]{2,1,0:T(1,128)S(1)}, u32[]{:S(2)}, u32[]{:S(2)}) async-start(f32[16,1,48]{2,1,0:T(1,128)} %compare_select_fusion), calls=%async_computation.2 | async-start | bytes 16384 | tf_op jit(solution)/shard_map/all_to_all | solution.py:69
  268.5 5.6 %select_select_fusion = s32[256]{0:T(256)S(1)} fusion(pred[256]{0:T(512)(128)(4,1)S(1)} %copy-done.22, pred[256]{0:T(512)(128)(4,1)S(1)} %copy-done.21, pred[256]{0:T(512)(128)(4,1)S(1)} %copy-done.20, pred[256]{0:T(512)(128)(4,1)S(1)} %copy-done.19, pred[256]{0:T(512)(128)(4,1)S(1)} %copy-done.18, pred[256]{0:T(512)(128)(4,1)S(1)} %copy-done.17, ...), kind=kLoop, calls=%fused_computation.84 | loop fusion | flops 2304 | bytes 4388 | tf_op jit(solution)/shard_map/gather | solution.py:70
  275.4 40.7 %psum.15 = f32[1024]{0:T(1024)S(1)} all-reduce(f32[1024]{0:T(1024)S(1)} %copy-done.10), channel_id=1, replica_groups=mesh['inner'=16,'outer'=2] {'inner','outer'}, use_global_device_ids=true, to_apply=%region_3.4 | all-reduce | flops 1024 | bytes 8192 | tf_op jit(solution)/shard_map/psum | solution.py:74
  316.2 1.9 gather_fusion.2
  319.4 1.8 subtract_divide_fusion
  (113 shorter events, 24.8 us)
Async XLA Ops:
  7.2 82.4 %copy-start = (bf16[1,256,2048]{2,1,0:T(8,128)(2,1)S(1)}, bf16[1,256,2048]{2,1,0:T(8,128)(2,1)}, u32[]{:S(2)}) copy-start(bf16[1,256,2048]{2,1,0:T(8,128)(2,1)} %param.6) | copy-start | bytes 3145732
  7.2 82.4 %all-gather.2.cloned.1.call-start = ((), (), s32[]{:S(2)}) async-start(), calls=%async_computation.3 | async-start | bytes 4456448 | tf_op jit(solution)/shard_map/all_gather | solution.py:39
  7.9 259.8 %reduce-scatter.2.cloned.1.call-start = ((), (), s32[]{:S(2)}) async-start(), calls=%async_computation.4 | async-start | bytes 4456448 | tf_op jit(solution)/shard_map/reduce_scatter | solution.py:77
  140.3 11.6 %all-to-all-start = ((s32[16,1,48]{2,1,0:T(1,128)}), s32[16,1,48]{2,1,0:T(1,128)S(1)}, u32[]{:S(2)}, u32[]{:S(2)}) async-start(s32[16,1,48]{2,1,0:T(1,128)} %bitcast.28), calls=%async_computation.1 | async-start | bytes 16384 | tf_op jit(solution)/shard_map/all_to_all | solution.py:64
  169.4 11.2 %copy-start.23 = (bf16[1,256,2048]{2,1,0:T(8,128)(2,1)S(1)}, bf16[1,256,2048]{2,1,0:T(8,128)(2,1)}, u32[]{:S(2)}) copy-start(bf16[1,256,2048]{2,1,0:T(8,128)(2,1)} %param.7) | copy-start | bytes 3145732
  170.6 85.3 %collective-permute-start.14 = (bf16[1,48,1024]{2,1,0:T(8,128)(2,1)}, bf16[1,48,1024]{2,1,0:T(8,128)(2,1)S(1)}, u32[]{:S(2)}, u32[]{:S(2)}) collective-permute-start(bf16[1,48,1024]{2,1,0:T(8,128)(2,1)} %get-tuple-element.15), channel_id=1, source_target_pairs={{0,30},{2,28},{4,26},{6,24},{8,22},{10,20},{12,18},{14,16},{16,14}... | collective-permute-start | bytes 294920 | tf_op jit(solution)/shard_map/ppermute | solution.py:25
  171.5 84.4 %collective-permute-start.13 = (bf16[1,48,1024]{2,1,0:T(8,128)(2,1)}, bf16[1,48,1024]{2,1,0:T(8,128)(2,1)S(1)}, u32[]{:S(2)}, u32[]{:S(2)}) collective-permute-start(bf16[1,48,1024]{2,1,0:T(8,128)(2,1)} %get-tuple-element.16), channel_id=1, source_target_pairs={{0,28},{2,30},{4,24},{6,26},{8,20},{10,22},{12,16},{14,18},{16,12}... | collective-permute-start | bytes 294920 | tf_op jit(solution)/shard_map/ppermute | solution.py:25
  175.4 80.4 %collective-permute-start.12 = (bf16[1,48,1024]{2,1,0:T(8,128)(2,1)}, bf16[1,48,1024]{2,1,0:T(8,128)(2,1)S(1)}, u32[]{:S(2)}, u32[]{:S(2)}) collective-permute-start(bf16[1,48,1024]{2,1,0:T(8,128)(2,1)} %get-tuple-element.17), channel_id=1, source_target_pairs={{0,26},{2,24},{4,30},{6,28},{8,18},{10,16},{12,22},{14,20},{16,10}... | collective-permute-start | bytes 294920 | tf_op jit(solution)/shard_map/ppermute | solution.py:25
  177.0 78.8 %collective-permute-start.11 = (bf16[1,48,1024]{2,1,0:T(8,128)(2,1)}, bf16[1,48,1024]{2,1,0:T(8,128)(2,1)S(1)}, u32[]{:S(2)}, u32[]{:S(2)}) collective-permute-start(bf16[1,48,1024]{2,1,0:T(8,128)(2,1)} %get-tuple-element.18), channel_id=1, source_target_pairs={{0,24},{2,26},{4,28},{6,30},{8,16},{10,18},{12,20},{14,22},{16,8},... | collective-permute-start | bytes 294920 | tf_op jit(solution)/shard_map/ppermute | solution.py:25
  180.0 9.4 %collective-permute-start = (bf16[1,48,1024]{2,1,0:T(8,128)(2,1)}, bf16[1,48,1024]{2,1,0:T(8,128)(2,1)}, u32[]{:S(2)}, u32[]{:S(2)}) collective-permute-start(bf16[1,48,1024]{2,1,0:T(8,128)(2,1)} %get-tuple-element.29), channel_id=1, source_target_pairs={{0,2},{2,0},{4,6},{6,4},{8,10},{10,8},{12,14},{14,12},{16,18},{18,... | collective-permute-start | bytes 294920 | tf_op jit(solution)/shard_map/ppermute | solution.py:25
  187.7 45.2 %copy-start.5 = (bf16[1,48,1024]{2,1,0:T(8,128)(2,1)S(1)}, bf16[1,48,1024]{2,1,0:T(8,128)(2,1)}, u32[]{:S(2)}) copy-start(bf16[1,48,1024]{2,1,0:T(8,128)(2,1)} %get-tuple-element.21) | copy-start | bytes 294916
  187.7 54.3 %copy-start.4 = (bf16[1,48,1024]{2,1,0:T(8,128)(2,1)S(1)}, bf16[1,48,1024]{2,1,0:T(8,128)(2,1)}, u32[]{:S(2)}) copy-start(bf16[1,48,1024]{2,1,0:T(8,128)(2,1)} %get-tuple-element.20) | copy-start | bytes 294916
  187.7 60.7 %copy-start.3 = (bf16[1,48,1024]{2,1,0:T(8,128)(2,1)S(1)}, bf16[1,48,1024]{2,1,0:T(8,128)(2,1)}, u32[]{:S(2)}) copy-start(bf16[1,48,1024]{2,1,0:T(8,128)(2,1)} %get-tuple-element.19) | copy-start | bytes 294916
  189.5 5.7 %collective-permute-start.1 = (bf16[1,48,1024]{2,1,0:T(8,128)(2,1)}, bf16[1,48,1024]{2,1,0:T(8,128)(2,1)S(1)}, u32[]{:S(2)}, u32[]{:S(2)}) collective-permute-start(bf16[1,48,1024]{2,1,0:T(8,128)(2,1)} %get-tuple-element.28), channel_id=1, source_target_pairs={{0,4},{2,6},{4,0},{6,2},{8,12},{10,14},{12,8},{14,10},{16,20},{18,... | collective-permute-start | bytes 294920 | tf_op jit(solution)/shard_map/ppermute | solution.py:25
  195.2 5.7 %collective-permute-start.2 = (bf16[1,48,1024]{2,1,0:T(8,128)(2,1)}, bf16[1,48,1024]{2,1,0:T(8,128)(2,1)S(1)}, u32[]{:S(2)}, u32[]{:S(2)}) collective-permute-start(bf16[1,48,1024]{2,1,0:T(8,128)(2,1)} %get-tuple-element.27), channel_id=1, source_target_pairs={{0,6},{2,4},{4,2},{6,0},{8,14},{10,12},{12,10},{14,8},{16,22},{18,... | collective-permute-start | bytes 294920 | tf_op jit(solution)/shard_map/ppermute | solution.py:25
  200.9 5.3 %collective-permute-start.3 = (bf16[1,48,1024]{2,1,0:T(8,128)(2,1)}, bf16[1,48,1024]{2,1,0:T(8,128)(2,1)S(1)}, u32[]{:S(2)}, u32[]{:S(2)}) collective-permute-start(bf16[1,48,1024]{2,1,0:T(8,128)(2,1)} %get-tuple-element.26), channel_id=1, source_target_pairs={{0,8},{2,10},{4,12},{6,14},{8,0},{10,2},{12,4},{14,6},{16,24},{18,... | collective-permute-start | bytes 294920 | tf_op jit(solution)/shard_map/ppermute | solution.py:25
  206.2 5.7 %collective-permute-start.4 = (bf16[1,48,1024]{2,1,0:T(8,128)(2,1)}, bf16[1,48,1024]{2,1,0:T(8,128)(2,1)S(1)}, u32[]{:S(2)}, u32[]{:S(2)}) collective-permute-start(bf16[1,48,1024]{2,1,0:T(8,128)(2,1)} %get-tuple-element.25), channel_id=1, source_target_pairs={{0,10},{2,8},{4,14},{6,12},{8,2},{10,0},{12,6},{14,4},{16,26},{18,... | collective-permute-start | bytes 294920 | tf_op jit(solution)/shard_map/ppermute | solution.py:25
  211.9 6.5 %collective-permute-start.5 = (bf16[1,48,1024]{2,1,0:T(8,128)(2,1)}, bf16[1,48,1024]{2,1,0:T(8,128)(2,1)S(1)}, u32[]{:S(2)}, u32[]{:S(2)}) collective-permute-start(bf16[1,48,1024]{2,1,0:T(8,128)(2,1)} %get-tuple-element.24), channel_id=1, source_target_pairs={{0,12},{2,14},{4,8},{6,10},{8,4},{10,6},{12,0},{14,2},{16,28},{18,... | collective-permute-start | bytes 294920 | tf_op jit(solution)/shard_map/ppermute | solution.py:25
  218.4 6.6 %collective-permute-start.6 = (bf16[1,48,1024]{2,1,0:T(8,128)(2,1)}, bf16[1,48,1024]{2,1,0:T(8,128)(2,1)S(1)}, u32[]{:S(2)}, u32[]{:S(2)}) collective-permute-start(bf16[1,48,1024]{2,1,0:T(8,128)(2,1)} %get-tuple-element.23), channel_id=1, source_target_pairs={{0,14},{2,12},{4,10},{6,8},{8,6},{10,4},{12,2},{14,0},{16,30},{18,... | collective-permute-start | bytes 294920 | tf_op jit(solution)/shard_map/ppermute | solution.py:25
  225.1 7.8 %collective-permute-start.7 = (bf16[1,48,1024]{2,1,0:T(8,128)(2,1)}, bf16[1,48,1024]{2,1,0:T(8,128)(2,1)S(1)}, u32[]{:S(2)}, u32[]{:S(2)}) collective-permute-start(bf16[1,48,1024]{2,1,0:T(8,128)(2,1)} %get-tuple-element.22), channel_id=1, source_target_pairs={{0,16},{2,18},{4,20},{6,22},{8,24},{10,26},{12,28},{14,30},{16,0},... | collective-permute-start | bytes 294920 | tf_op jit(solution)/shard_map/ppermute | solution.py:25
  232.9 9.1 %collective-permute-start.8 = (bf16[1,48,1024]{2,1,0:T(8,128)(2,1)S(1)}, bf16[1,48,1024]{2,1,0:T(8,128)(2,1)S(1)}, u32[]{:S(2)}, u32[]{:S(2)}) collective-permute-start(bf16[1,48,1024]{2,1,0:T(8,128)(2,1)S(1)} %copy-done.5), channel_id=1, source_target_pairs={{0,18},{2,16},{4,22},{6,20},{8,26},{10,24},{12,30},{14,28},{16,2},... | collective-permute-start | bytes 294920 | tf_op jit(solution)/shard_map/ppermute | solution.py:25
  242.0 6.4 %collective-permute-start.9 = (bf16[1,48,1024]{2,1,0:T(8,128)(2,1)S(1)}, bf16[1,48,1024]{2,1,0:T(8,128)(2,1)S(1)}, u32[]{:S(2)}, u32[]{:S(2)}) collective-permute-start(bf16[1,48,1024]{2,1,0:T(8,128)(2,1)S(1)} %copy-done.4), channel_id=1, source_target_pairs={{0,20},{2,22},{4,16},{6,18},{8,28},{10,30},{12,24},{14,26},{16,4},... | collective-permute-start | bytes 294920 | tf_op jit(solution)/shard_map/ppermute | solution.py:25
  248.4 7.3 %collective-permute-start.10 = (bf16[1,48,1024]{2,1,0:T(8,128)(2,1)S(1)}, bf16[1,48,1024]{2,1,0:T(8,128)(2,1)S(1)}, u32[]{:S(2)}, u32[]{:S(2)}) collective-permute-start(bf16[1,48,1024]{2,1,0:T(8,128)(2,1)S(1)} %copy-done.3), channel_id=1, source_target_pairs={{0,22},{2,20},{4,18},{6,16},{8,30},{10,28},{12,26},{14,24},{16,6},... | collective-permute-start | bytes 294920 | tf_op jit(solution)/shard_map/ppermute | solution.py:25
  260.6 7.8 %copy-start.16 = (pred[256]{0:T(512)(128)(4,1)S(1)}, pred[256]{0:T(512)(128)(4,1)}, u32[]{:S(2)}) copy-start(pred[256]{0:T(512)(128)(4,1)} %get-tuple-element.4) | copy-start | bytes 772
  260.6 7.8 %copy-start.17 = (pred[256]{0:T(512)(128)(4,1)S(1)}, pred[256]{0:T(512)(128)(4,1)}, u32[]{:S(2)}) copy-start(pred[256]{0:T(512)(128)(4,1)} %get-tuple-element.5) | copy-start | bytes 772
  260.6 7.8 %copy-start.18 = (pred[256]{0:T(512)(128)(4,1)S(1)}, pred[256]{0:T(512)(128)(4,1)}, u32[]{:S(2)}) copy-start(pred[256]{0:T(512)(128)(4,1)} %get-tuple-element.6) | copy-start | bytes 772
  260.6 7.8 %copy-start.19 = (pred[256]{0:T(512)(128)(4,1)S(1)}, pred[256]{0:T(512)(128)(4,1)}, u32[]{:S(2)}) copy-start(pred[256]{0:T(512)(128)(4,1)} %get-tuple-element.7) | copy-start | bytes 772
  260.7 13.5 %copy-start.13 = (s32[2,16]{1,0:T(2,128)S(1)}, s32[2,16]{1,0:T(2,128)}, u32[]{:S(2)}) copy-start(s32[2,16]{1,0:T(2,128)} %param.9) | copy-start | bytes 388
  260.7 14.7 %copy-start.10 = (f32[1024]{0:T(1024)S(1)}, f32[1024]{0:T(1024)}, u32[]{:S(2)}) copy-start(f32[1024]{0:T(1024)} %get-tuple-element.46) | copy-start | bytes 12292
  262.7 55.5 %copy-start.9 = (s32[1,256]{1,0:T(1,128)S(1)}, s32[1,256]{1,0:T(1,128)}, u32[]{:S(2)}) copy-start(s32[1,256]{1,0:T(1,128)} %param.11) | copy-start | bytes 3076
  264.0 52.2 %all-to-all-start.1 = ((f32[16,1,48]{2,1,0:T(1,128)}), f32[16,1,48]{2,1,0:T(1,128)S(1)}, u32[]{:S(2)}, u32[]{:S(2)}) async-start(f32[16,1,48]{2,1,0:T(1,128)} %compare_select_fusion), calls=%async_computation.2 | async-start | bytes 16384 | tf_op jit(solution)/shard_map/all_to_all | solution.py:69
  267.7 51.7 %all-reduce.2.cloned.1.call-start = ((), (), s32[]{:S(2)}) async-start(), calls=%async_computation.5 | async-start | bytes 524288 | tf_op jit(solution)/shard_map/psum | solution.py:85
  (12 other events, 65.6 us)
Sparse Core Ops, SparseCore 0:
  10.8 78.7 all-gather.1
  96.6 100.2 reduce-scatter.1
  270.8 19.5 all-reduce.1
